TPU v7x, 32 devices: a whole 2x2x4 slice. The times are simulated.
32 devices in a mesh: tm: 16 (over z, x, core), panel: 2 (over y).
Axes of the slice: x: 2, y: 2, z: 4, core: 2. Of those that a mesh axis runs over, the one named last changes fastest.
Arguments:
- observations: bfloat16 [4096, 8192], P('panel', 'tm'), may hold values from -6 to 6
- info_weight: bfloat16 [4096, 1024], P('panel'), may hold values from -0.09375 to 0.09375
- readout: bfloat16 [4096, 1024], P('panel'), may hold values from -0.1875 to 0.1875
- labels: int32 [8192], P('tm'), may hold values from 0 to 3
- rate: float32 [4, 512], P(None, 'panel'), as said below
- angle: float32 [4, 512], P(None, 'panel'), may hold values from -0.3 to 0.3
- gain: float32 [4, 512], P(None, 'panel'), may hold values from 0.5 to 2
Outputs:
- smoothed: float32 [1024, 8192], P('panel', 'tm')
- predicted: bfloat16 [4096, 8192], P('panel', 'tm')
Inputs may be any that keep to these rules, and one draw needn't show every extreme that they name: `rate`: every entry is positive.
All inputs are finite; a program needn't handle non-finite values.
Results may differ from a plain program's by a relative error of at most 0.013.
Values may be sent and summed in bfloat16 or wider, within the bound.
A program may use at most 128 MiB of HBM per device.

v0:
```python
import jax
import jax.numpy as jnp
from jax import lax
from jax.sharding import PartitionSpec as P

REGION_LATENT = 128


def from_behind(shard, axis, by):
    devices = lax.axis_size(axis)
    pairs = [(i, i + by) for i in range(devices) if 0 <= i + by < devices]
    return lax.ppermute(shard, axis, pairs)


def entering(value, axis, join, neutral, backward):
    count, mine = (lax.axis_size(axis), lax.axis_index(axis))
    pieces = jax.tree.map(lambda part: lax.all_gather(part, axis), value)
    if backward:
        pieces = jax.tree.map(lambda part: part[::-1], pieces)
        mine = count - 1 - mine
    so_far = jax.tree.map(
        lambda part, zero: jnp.full_like(part, 0) + jnp.asarray(zero, part.dtype), value, neutral
    )

    def step(position, so_far):
        longer = join(so_far, jax.tree.map(lambda part: part[position], pieces))
        return jax.tree.map(lambda new, old: jnp.where(position < mine, new, old), longer, so_far)

    return lax.fori_loop(0, count - 1, step, so_far)


def compose(earlier, later):
    ere, eim, ebr, ebi = earlier
    lre, lim, lbr, lbi = later
    return (
        lre * ere - lim * eim,
        lre * eim + lim * ere,
        lre * ebr - lim * ebi + lbr,
        lre * ebi + lim * ebr + lbi,
    )


def select(table, regime):
    result = jnp.zeros((table.shape[1], regime.shape[0]), jnp.float32)
    for which in range(table.shape[0]):
        result = jnp.where(regime[None, :] == which, table[which][:, None], result)
    return result


def body(observations, info_weight, readout, labels, rate, angle, gain):
    bins = observations.shape[1]
    lat_dev = info_weight.shape[1] // lax.axis_size("panel")
    half = REGION_LATENT // 2
    areas_dev = lat_dev // REGION_LATENT
    pair_dev = rate.shape[1]
    columns = lax.all_to_all(info_weight, "panel", split_axis=1, concat_axis=0, tiled=True)
    cols = columns
    info = lax.dot_general(
        cols,
        lax.all_gather(observations, "panel", axis=0, tiled=True),
        (((0,), (0,)), ((), ())),
        preferred_element_type=jnp.float32,
    )
    view = info.reshape(areas_dev, 2, half, bins)
    zre = view[:, 0].reshape(pair_dev, bins)
    zim = view[:, 1].reshape(pair_dev, bins)
    lam = select(rate, labels)
    ang = select(angle, labels)
    scale = select(gain, labels) * jnp.sqrt(-jnp.expm1(-2.0 * lam))
    mag = jnp.exp(-lam)
    are = mag * jnp.cos(ang)
    aim = mag * jnp.sin(ang)
    prod_re, prod_im, loc_re, loc_im = lax.associative_scan(
        compose, (are, aim, scale * zre, scale * zim), axis=1
    )
    arriving = from_behind(labels[:1], "tm", -1)
    following = jnp.concatenate([labels[1:], arriving])
    lam_next = select(rate, following)
    ang_next = select(angle, following)
    mag_next = jnp.exp(-lam_next)
    is_last = lax.axis_index("tm") == lax.axis_size("tm") - 1
    final = jnp.logical_and(is_last, lax.iota(jnp.int32, bins) == bins - 1)[None, :]
    gre = jnp.where(final, 0.0, mag_next * jnp.cos(ang_next))
    gim = jnp.where(final, 0.0, -(mag_next * jnp.sin(ang_next)))
    coef = jnp.where(final, 1.0, -jnp.expm1(-2.0 * lam_next))
    ones = jnp.ones((pair_dev,), jnp.float32)
    zeros = jnp.zeros((pair_dev,), jnp.float32)
    before = entering(
        (prod_re[:, -1], prod_im[:, -1], loc_re[:, -1], loc_im[:, -1]),
        "tm",
        compose,
        (ones, zeros, zeros, zeros),
        False,
    )
    in_re, in_im = (before[2][:, None], before[3][:, None])
    mre = loc_re + prod_re * in_re - prod_im * in_im
    mim = loc_im + prod_re * in_im + prod_im * in_re
    sum_re, sum_im, back_re, back_im = lax.associative_scan(
        compose, (gre, gim, coef * mre, coef * mim), reverse=True, axis=1
    )
    after = entering(
        (sum_re[:, 0], sum_im[:, 0], back_re[:, 0], back_im[:, 0]),
        "tm",
        compose,
        (ones, zeros, zeros, zeros),
        True,
    )
    out_re, out_im = (after[2][:, None], after[3][:, None])
    sre = back_re + sum_re * out_re - sum_im * out_im
    sim = back_im + sum_re * out_im + sum_im * out_re
    smoothed = jnp.stack(
        [sre.reshape(areas_dev, half, bins), sim.reshape(areas_dev, half, bins)], 1
    ).reshape(lat_dev, bins)
    smoothed_half = smoothed.astype(jnp.bfloat16)
    cols = readout
    predicted = jnp.dot(
        cols,
        lax.all_gather(smoothed_half, "panel", axis=0, tiled=True),
        preferred_element_type=jnp.float32,
    )
    return (smoothed, predicted.astype(jnp.bfloat16))


def solution(mesh):
    return jax.shard_map(
        body,
        mesh=mesh,
        in_specs=(
            P("panel", "tm"),
            P("panel", None),
            P("panel", None),
            P("tm"),
            P(None, "panel"),
            P(None, "panel"),
            P(None, "panel"),
        ),
        out_specs=(P("panel", "tm"), P("panel", "tm")),
        check_vma=False,
    )
```

profile of v0, /device:TPU:0, one launch (start us, length us, event | category | flops | bytes accessed | tf_op | source)
XLA Modules:
  0.0 1554.3 jit_solution(15167774816155730735)
XLA Ops:
  35.6 12.2 slice.1359
  47.8 12.2 slice.1368
  60.0 12.2 slice.1355
  72.2 12.1 slice.1366
  84.4 12.2 slice.1307
  119.9 12.3 slice.1180
  168.6 11.9 slice.1488
  209.5 12.2 slice.1350
  233.3 12.6 slice.1186
  245.9 12.2 slice.1182
  258.1 12.2 slice.1194
  449.1 12.5 slice.1311
  653.1 35.4 %all-gather = f32[4096,1]{1,0:T(8,128)S(1)} all-gather(f32[256,1]{1,0:T(8,128)S(1)} %slice_add_fusion.45), channel_id=2, replica_groups=mesh['tm'=16,'panel'=2] {'tm'}, dimensions={0}, use_global_device_ids=true | all-gather | bytes 17408 | tf_op jit(solution)/shard_map/all_gather | solution.py:17
  710.6 30.1 %all-gather.1 = f32[4096,1]{1,0:T(8,128)S(1)} all-gather(f32[256,1]{1,0:T(8,128)S(1)} %slice_add_fusion.44), channel_id=3, replica_groups=mesh['tm'=16,'panel'=2] {'tm'}, dimensions={0}, use_global_device_ids=true | all-gather | bytes 17408 | tf_op jit(solution)/shard_map/all_gather | solution.py:17
  761.5 30.2 %all-gather.2 = f32[4096,1]{1,0:T(8,128)S(1)} all-gather(f32[256,1]{1,0:T(8,128)S(1)} %slice_add_fusion.43), channel_id=4, replica_groups=mesh['tm'=16,'panel'=2] {'tm'}, dimensions={0}, use_global_device_ids=true | all-gather | bytes 17408 | tf_op jit(solution)/shard_map/all_gather | solution.py:17
  792.5 28.0 %all-gather.3 = f32[4096,1]{1,0:T(8,128)S(1)} all-gather(f32[256,1]{1,0:T(8,128)S(1)} %slice_add_fusion.42), channel_id=5, replica_groups=mesh['tm'=16,'panel'=2] {'tm'}, dimensions={0}, use_global_device_ids=true | all-gather | bytes 17408 | tf_op jit(solution)/shard_map/all_gather | solution.py:17
  870.8 12.1 slice.1374
  1074.4 12.2 slice.1493
  1088.9 12.4 slice.1533
  1389.9 28.4 %all-gather.4 = f32[4096,1]{1,0:T(8,128)S(1)} all-gather(f32[256,1]{1,0:T(8,128)S(1)} %slice_add_fusion.11), channel_id=6, replica_groups=mesh['tm'=16,'panel'=2] {'tm'}, dimensions={0}, use_global_device_ids=true | all-gather | bytes 17408 | tf_op jit(solution)/shard_map/all_gather | solution.py:17
  1419.1 30.3 %all-gather.5 = f32[4096,1]{1,0:T(8,128)S(1)} all-gather(f32[256,1]{1,0:T(8,128)S(1)} %copy-done.63), channel_id=7, replica_groups=mesh['tm'=16,'panel'=2] {'tm'}, dimensions={0}, use_global_device_ids=true | all-gather | bytes 17408 | tf_op jit(solution)/shard_map/all_gather | solution.py:17
  1450.0 28.9 %all-gather.6 = f32[4096,1]{1,0:T(8,128)S(1)} all-gather(f32[256,1]{1,0:T(8,128)S(1)} %copy-done.64), channel_id=8, replica_groups=mesh['tm'=16,'panel'=2] {'tm'}, dimensions={0}, use_global_device_ids=true | all-gather | bytes 17408 | tf_op jit(solution)/shard_map/all_gather | solution.py:17
  1479.7 30.0 %all-gather.7 = f32[4096,1]{1,0:T(8,128)S(1)} all-gather(f32[256,1]{1,0:T(8,128)S(1)} %copy-done.65), channel_id=9, replica_groups=mesh['tm'=16,'panel'=2] {'tm'}, dimensions={0}, use_global_device_ids=true | all-gather | bytes 17408 | tf_op jit(solution)/shard_map/all_gather | solution.py:17
  1515.1 24.8 %all-gather.13.cloned.1.call-done = bf16[1024,512]{1,0:T(8,128)(2,1)} async-done(((bf16[512,512]{1,0:T(8,128)(2,1)}), bf16[1024,512]{1,0:T(8,128)(2,1)}) %all-gather.13.cloned.1.call-update) | async-done | bytes 1048592 | tf_op jit(solution)/shard_map/all_gather | solution.py:118
  (1035 shorter events, 1098.8 us)
Async XLA Ops:
  7.2 195.3 %all-gather.11.cloned.1.call-start = ((), (), s32[]{:S(2)}) async-start(), calls=%async_computation.1 | async-start | bytes 6291456 | tf_op jit(solution)/shard_map/all_gather | solution.py:60
  20.7 175.3 %all-to-all-start = ((bf16[2048,2,512]{2,0,1:T(8,128)(2,1)}), bf16[2048,2,512]{2,0,1:T(8,128)(2,1)}, u32[]{:S(2)}, u32[]{:S(2)}) async-start(bf16[2048,2,512]{2,0,1:T(8,128)(2,1)} %copy.345), calls=%async_computation | async-start | bytes 8388608 | tf_op jit(solution)/shard_map/all_to_all | solution.py:56
  26.8 1513.1 %all-gather.13.cloned.1.call-start = ((), (), s32[]{:S(2)}) async-start(), calls=%async_computation.2 | async-start | bytes 1572864 | tf_op jit(solution)/shard_map/all_gather | solution.py:118
  27.3 3.1 collective-permute-start
  28.7 55.6 %copy-start.118 = (pred[512]{0:T(512)(128)(4,1)}, pred[512]{0:T(512)(128)(4,1)S(1)}, u32[]{:S(2)}) copy-start(pred[512]{0:T(512)(128)(4,1)S(1)} %fusion.35) | copy-start | bytes 1540
  28.8 179.5 %copy-start.98 = (f32[1,256]{1,0:T(1,128)}, f32[1,256]{1,0:T(1,128)S(1)}, u32[]{:S(2)}) copy-start(f32[1,256]{1,0:T(1,128)S(1)} %get-tuple-element.684) | copy-start | bytes 3076
  28.8 179.5 %copy-start.100 = (f32[1,256]{1,0:T(1,128)}, f32[1,256]{1,0:T(1,128)S(1)}, u32[]{:S(2)}) copy-start(f32[1,256]{1,0:T(1,128)S(1)} %get-tuple-element.685) | copy-start | bytes 3076
  28.8 179.5 %copy-start.102 = (f32[1,256]{1,0:T(1,128)}, f32[1,256]{1,0:T(1,128)S(1)}, u32[]{:S(2)}) copy-start(f32[1,256]{1,0:T(1,128)S(1)} %get-tuple-element.686) | copy-start | bytes 3076
  28.8 179.5 %copy-start.104 = (f32[1,256]{1,0:T(1,128)}, f32[1,256]{1,0:T(1,128)S(1)}, u32[]{:S(2)}) copy-start(f32[1,256]{1,0:T(1,128)S(1)} %get-tuple-element.687) | copy-start | bytes 3076
  31.2 53.2 %copy-start.111 = (pred[512]{0:T(512)(128)(4,1)}, pred[512]{0:T(512)(128)(4,1)S(1)}, u32[]{:S(2)}) copy-start(pred[512]{0:T(512)(128)(4,1)S(1)} %get-tuple-element.694) | copy-start | bytes 1540
  31.2 53.2 %copy-start.113 = (pred[512]{0:T(512)(128)(4,1)}, pred[512]{0:T(512)(128)(4,1)S(1)}, u32[]{:S(2)}) copy-start(pred[512]{0:T(512)(128)(4,1)S(1)} %get-tuple-element.695) | copy-start | bytes 1540
  271.5 61.6 %copy-start.28 = (f32[256,256]{1,0:T(8,128)}, f32[256,256]{1,0:T(8,128)S(1)}, u32[]{:S(2)}) copy-start(f32[256,256]{1,0:T(8,128)S(1)} %get-tuple-element.516) | copy-start | bytes 786436
  271.6 65.8 %copy-start.21 = (f32[256,256]{1,0:T(8,128)}, f32[256,256]{1,0:T(8,128)S(1)}, u32[]{:S(2)}) copy-start(f32[256,256]{1,0:T(8,128)S(1)} %get-tuple-element.416) | copy-start | bytes 786436
  403.1 60.7 %copy-start.22 = (f32[256,256]{1,0:T(8,128)S(1)}, f32[256,256]{1,0:T(8,128)}, u32[]{:S(2)}) copy-start(f32[256,256]{1,0:T(8,128)} %copy-done.21) | copy-start | bytes 786436
  623.3 76.1 %copy-start.67 = (f32[256,1]{1,0:T(8,128)S(1)}, f32[256,1]{1,0:T(8,128)}, u32[]{:S(2)}) copy-start(f32[256,1]{1,0:T(8,128)} %slice.1646) | copy-start | bytes 3076
  761.5 59.7 %copy-start.96 = (f32[256]{0:T(256)S(1)}, f32[256]{0:T(256)}, u32[]{:S(2)}) copy-start(f32[256]{0:T(256)} %custom-call) | copy-start | bytes 3076
  761.5 59.7 %copy-start.97 = (f32[256]{0:T(256)S(1)}, f32[256]{0:T(256)}, u32[]{:S(2)}) copy-start(f32[256]{0:T(256)} %custom-call.1) | copy-start | bytes 3076
  832.9 55.1 %copy-start.54 = (f32[256,256]{1,0:T(8,128)S(1)}, f32[256,256]{1,0:T(8,128)}, u32[]{:S(2)}) copy-start(f32[256,256]{1,0:T(8,128)} %slice.1360) | copy-start | bytes 786436
  889.2 61.6 %copy-start.30 = (f32[256,256]{1,0:T(8,128)}, f32[256,256]{1,0:T(8,128)S(1)}, u32[]{:S(2)}) copy-start(f32[256,256]{1,0:T(8,128)S(1)} %get-tuple-element.484) | copy-start | bytes 786436
  889.2 65.4 %copy-start.24 = (f32[256,256]{1,0:T(8,128)}, f32[256,256]{1,0:T(8,128)S(1)}, u32[]{:S(2)}) copy-start(f32[256,256]{1,0:T(8,128)S(1)} %get-tuple-element.412) | copy-start | bytes 786436
  1389.9 60.1 %copy-start.64 = (f32[256,1]{1,0:T(8,128)S(1)}, f32[256,1]{1,0:T(8,128)}, u32[]{:S(2)}) copy-start(f32[256,1]{1,0:T(8,128)} %slice_add_fusion.9) | copy-start | bytes 3076
  1419.1 60.6 %copy-start.65 = (f32[256,1]{1,0:T(8,128)S(1)}, f32[256,1]{1,0:T(8,128)}, u32[]{:S(2)}) copy-start(f32[256,1]{1,0:T(8,128)} %slice_add_fusion.8) | copy-start | bytes 3076
  1450.0 60.5 %copy-start.94 = (f32[256]{0:T(256)S(1)}, f32[256]{0:T(256)}, u32[]{:S(2)}) copy-start(f32[256]{0:T(256)} %custom-call.2) | copy-start | bytes 3076
  1450.0 60.5 %copy-start.95 = (f32[256]{0:T(256)S(1)}, f32[256]{0:T(256)}, u32[]{:S(2)}) copy-start(f32[256]{0:T(256)} %custom-call.3) | copy-start | bytes 3076
  (100 other events, 2424.8 us)
Sparse Core Ops, SparseCore 0:
  9.5 97.5 all-gather.10
  1515.2 24.6 all-gather.12
where the time goes:
time: 1570 us; the launch traced here: 1550 us
  local copies, waits for them, and re-layouts  1120 us (71%)
  blocking collectives  241 us (15%)
  other arithmetic  131 us (8%)
  waiting for transfers between devices  27.1 us (2%)
  between operations  18 us (1%)
    slice x110, local copies, waits for them, and re-layouts, body(): lax.associative_scan(compose, (gre, gim, coef * mre, coef * mim), reverse...  330 us
    slice x101, local copies, waits for them, and re-layouts, body(): lax.associative_scan(compose, (are, aim, scale * zre, scale * zim), axis=1)  313 us
    all_gather x8, blocking collectives, entering(): pieces = jax.tree.map(lambda part: lax.all_gather(part, axis), value)  241 us
    pad x64, local copies, waits for them, and re-layouts, body(): lax.associative_scan(compose, (gre, gim, coef * mre, coef * mim), reverse...  178 us
    pad x64, local copies, waits for them, and re-layouts, body(): lax.associative_scan(compose, (are, aim, scale * zre, scale * zim), axis=1)  160 us
    unnamed x282, local copies, waits for them, and re-layouts  43.3 us
  transfers between devices with their start and end apart: 4, of which 2 were waited for; matrix products, arithmetic and copies ran while one was open for 12% of the time, Pallas kernels for 0%

commit v1 on v0

v1 whole, which is shorter than its diff:
```python
import functools

import jax
import jax.numpy as jnp
from jax import lax
from jax.experimental import pallas as pl
from jax.experimental.pallas import tpu as pltpu
from jax.sharding import PartitionSpec as P

LANES = 128
HALF = 64
CHUNKS = 8
ROWS = 16
MESH = pl.DeviceIdType.MESH


def mul(x, y):
    return x[0] * y[0] - x[1] * y[1], x[0] * y[1] + x[1] * y[0]


def cmul(x, y):
    return x[0] * y[0] + x[1] * y[1], x[0] * y[1] - x[1] * y[0]


def add(x, y):
    return x[0] + y[0], x[1] + y[1]


def smooth_kernel(
    n, pn, groups, gw, regimes,
    obs_hbm, w_hbm, lab_ref, tab_ref,
    sm_hbm, sh_hbm,
    obs, obs_t, w, own, rs_out, rs_in, xre, xim, are, aim, coef, mre, mim, pre, pim,
    chunk, msgs, enter, bound, smv, shv,
    in_sem, rs_send, rs_recv, cm_send, cm_recv, ag_send, ag_recv, out_sem,
):
    me = lax.axis_index("tm")
    mp = lax.axis_index("panel")
    units, bins = obs.shape
    lat = own.shape[1]
    steps = bins // CHUNKS
    wide = gw == 2 * LANES

    def panel(s):
        return lax.rem(mp + s, pn)

    obs_copy = pltpu.make_async_copy(obs_hbm, obs, in_sem.at[0])
    obs_copy.start()
    w_copies = {}
    for s in list(range(1, pn)) + [0]:
        columns = pl.ds(pl.multiple_of(panel(s) * lat, LANES), lat)
        w_copies[s] = pltpu.make_async_copy(w_hbm.at[:, columns], w.at[s], in_sem.at[1 + s])
        w_copies[s].start()

    barrier = pltpu.get_barrier_semaphore()

    for s in range(1, pn):
        pl.semaphore_signal(barrier, inc=1, device_id=(me, panel(s)), device_id_type=MESH)

    def greet(s, _):
        pl.semaphore_signal(
            barrier, inc=1, device_id=(lax.rem(me + s, n), mp), device_id_type=MESH
        )
        return 0

    lax.fori_loop(1, n, greet, 0)

    obs_copy.wait()
    tile = 256

    def turn(i, _):
        rows = pl.ds(pl.multiple_of(i * tile, tile), tile)
        obs_t[:, rows] = obs[rows, :].T
        return 0

    lax.fori_loop(0, units // tile, turn, 0)

    def rs_copy(g, s):
        return pltpu.make_async_remote_copy(
            src_ref=rs_out.at[g, s - 1], dst_ref=rs_in.at[g, s - 1],
            send_sem=rs_send.at[g, s - 1], recv_sem=rs_recv.at[g, s - 1],
            device_id=(me, panel(s)), device_id_type=MESH,
        )

    def project(g, s):
        return jnp.dot(
            obs_t[...], w[s, :, g * gw:(g + 1) * gw], preferred_element_type=jnp.float32
        )

    for s in range(1, pn):
        w_copies[s].wait()
    for g in range(groups):
        for s in range(1, pn):
            rs_out[g, s - 1] = project(g, s).astype(jnp.bfloat16)
            if g == 0 and s == 1:
                pl.semaphore_wait(barrier, n - 1 + pn - 1)
            rs_copy(g, s).start()
    w_copies[0].wait()
    for g in range(groups):
        own[:, g * gw:(g + 1) * gw] = project(g, 0)

    lane = lax.broadcasted_iota(jnp.int32, (bins, LANES), 1)
    low = lane < HALF

    def swap(x):
        return pltpu.roll(x, HALF, 1)

    def gather_info(g):
        for s in range(1, pn):
            rs_copy(g, s).wait_recv()
        parts = []
        for h in range(gw // LANES):
            x = own[:, g * gw + h * LANES:g * gw + (h + 1) * LANES]
            for s in range(1, pn):
                x = x + rs_in[g, s - 1, :, h * LANES:(h + 1) * LANES].astype(jnp.float32)
            parts.append(x)
        if wide:
            xre[g] = jnp.where(low, parts[0], swap(parts[1]))
            xim[g] = jnp.where(low, swap(parts[0]), parts[1])
        else:
            xre[g] = parts[0]
            xim[g] = swap(parts[0])

    def rows_of(k):
        return pl.ds(pl.multiple_of(k * CHUNKS, CHUNKS), CHUNKS)

    def forward(g):
        def row(q, r):
            return jnp.broadcast_to(
                tab_ref[q * regimes + r:q * regimes + r + 1, g * LANES:(g + 1) * LANES],
                (CHUNKS, LANES),
            )

        table = [[row(q, r) for r in range(regimes)] for q in range(4)]

        def step(k, carry):
            m, p = carry
            rows = rows_of(k)
            label = lab_ref[rows, :]
            which = [label == r for r in range(regimes)]

            def pick(q):
                value = table[q][0]
                for r in range(1, regimes):
                    value = jnp.where(which[r], table[q][r], value)
                return value

            a = (pick(0), pick(1))
            scale, c = pick(2), pick(3)
            bin_rows = pl.ds(k, CHUNKS, stride=steps)
            u = (scale * xre[g, bin_rows, :], scale * xim[g, bin_rows, :])
            m = add(mul(a, m), u)
            p = mul(a, p)
            are[g, rows, :], aim[g, rows, :], coef[g, rows, :] = a[0], a[1], c
            mre[g, rows, :], mim[g, rows, :] = m
            pre[g, rows, :], pim[g, rows, :] = p
            return m, p

        zero = jnp.zeros((CHUNKS, LANES), jnp.float32)
        one = jnp.ones((CHUNKS, LANES), jnp.float32)
        return lax.fori_loop(0, steps, step, ((zero, zero), (one, zero)), unroll=4)

    def backward(g):
        def step(i, carry):
            e, d, w_ = carry
            k = steps - 2 - i
            rows, after = rows_of(k), rows_of(k + 1)
            a = (are[g, after, :], aim[g, after, :])
            c = coef[g, after, :]
            e = add(cmul(a, e), (c * mre[g, rows, :], c * mim[g, rows, :]))
            d = add(cmul(a, d), (c * pre[g, rows, :], c * pim[g, rows, :]))
            return e, d, cmul(a, w_)

        zero = jnp.zeros((CHUNKS, LANES), jnp.float32)
        one = jnp.ones((CHUNKS, LANES), jnp.float32)
        return lax.fori_loop(
            0, steps - 1, step, ((zero, zero), (zero, zero), (one, zero)), unroll=3
        )

    def chunk_row(g, q, c):
        return chunk[g, q, c:c + 1, :]

    def chunk_map(g, c):
        v = [chunk_row(g, q, c) for q in range(13)]
        return (v[0], v[1]), (v[2], v[3]), (v[4], v[5]), (v[6], v[7]), (v[8], v[9]), (v[10], v[11]), v[12]

    def local_map(g):
        b, a = forward(g)
        e, d, w_ = backward(g)
        first = rows_of(0)
        parts = (*a, *b, *w_, *e, *d, are[g, first, :], aim[g, first, :], coef[g, first, :])
        for q in range(13):
            chunk[g, q] = parts[q]
        A, B, G, E, D, a0, c0 = chunk_map(g, 0)
        for c in range(1, CHUNKS):
            Ar, Br, Gr, Er, Dr, ar, cr = chunk_map(g, c)
            K = cmul(ar, Dr)
            K = (K[0] + cr, K[1])
            E = add(E, mul(G, add(cmul(ar, Er), mul(K, B))))
            D = add(D, mul(G, mul(K, A)))
            G = mul(G, cmul(ar, Gr))
            A, B = mul(Ar, A), add(mul(Ar, B), Br)
        rows = (*A, *B, *G, *E, *D, *a0, c0)
        for q in range(13):
            msgs[g, 0, q:q + 1, :] = rows[q]
        msgs[g, 0, 13:ROWS, :] = jnp.zeros((ROWS - 13, LANES), jnp.float32)

    def cm_copy(g, s):
        return pltpu.make_async_remote_copy(
            src_ref=msgs.at[g, 0], dst_ref=msgs.at[g, s],
            send_sem=cm_send.at[g, s], recv_sem=cm_recv.at[g, s],
            device_id=(lax.rem(me + s, n), mp), device_id_type=MESH,
        )

    def each_peer(act):
        def go(s, _):
            act(s)
            return 0

        lax.fori_loop(1, n, go, 0)

    def boundary(g):
        zero = jnp.zeros((1, LANES), jnp.float32)

        def pair(slot, q):
            return msgs[g, slot, q:q + 1, :], msgs[g, slot, q + 1:q + 2, :]

        def put(d, row, value):
            enter[g, d, row:row + 1, :], enter[g, d, row + 1:row + 2, :] = value

        def get(d, row):
            return enter[g, d, row:row + 1, :], enter[g, d, row + 1:row + 2, :]

        def ahead(d, m):
            slot = lax.rem(me - d + n, n)
            put(d, 0, m)
            return add(mul(pair(slot, 0), m), pair(slot, 2))

        last = lax.fori_loop(0, n, ahead, (zero, zero))

        def back(i, s):
            d = n - 1 - i
            slot = lax.rem(me - d + n, n)
            put(d, 2, s)
            m = get(d, 0)
            first = add(add(mul(pair(slot, 4), s), pair(slot, 6)), mul(pair(slot, 8), m))
            c = msgs[g, slot, 12:13, :]
            return add(cmul(pair(slot, 10), first), (c * m[0], c * m[1]))

        lax.fori_loop(0, n, back, last)
        m_in, s_in = get(me, 0), get(me, 2)
        return m_in, s_in

    def finish(g):
        m, s = boundary(g)
        entering = []
        for c in range(CHUNKS):
            entering.append(m)
            bound[g, 0, c:c + 1, :], bound[g, 1, c:c + 1, :] = m
            A, B = chunk_map(g, c)[:2]
            m = add(mul(A, m), B)
        for c in reversed(range(CHUNKS)):
            bound[g, 2, c:c + 1, :], bound[g, 3, c:c + 1, :] = s
            _, _, G, E, D, a0, c0 = chunk_map(g, c)
            m = entering[c]
            first = add(add(mul(G, s), E), mul(D, m))
            s = add(cmul(a0, first), (c0 * m[0], c0 * m[1]))
        m_in = (bound[g, 0], bound[g, 1])
        s_in = (bound[g, 2], bound[g, 3])
        end = pl.ds(steps - 1, CHUNKS, stride=steps)
        xre[g, end, :], xim[g, end, :] = s_in

        def step(i, s):
            k = steps - 2 - i
            rows, after = rows_of(k), rows_of(k + 1)
            a = (are[g, after, :], aim[g, after, :])
            c = coef[g, after, :]
            m = add((mre[g, rows, :], mim[g, rows, :]), mul((pre[g, rows, :], pim[g, rows, :]), m_in))
            s = add(cmul(a, s), (c * m[0], c * m[1]))
            bin_rows = pl.ds(k, CHUNKS, stride=steps)
            xre[g, bin_rows, :], xim[g, bin_rows, :] = s
            return s

        lax.fori_loop(0, steps - 1, step, s_in, unroll=3)
        re, im = xre[g], xim[g]
        parts = [jnp.where(low, re, swap(im))]
        if wide:
            parts.append(jnp.where(low, swap(re), im))
        for h, x in enumerate(parts):
            smv[g, :, h * LANES:(h + 1) * LANES] = x
            shv[g, :, h * LANES:(h + 1) * LANES] = x.astype(jnp.bfloat16)

    def ag_copy(g, s):
        return pltpu.make_async_remote_copy(
            src_ref=shv.at[g], dst_ref=sh_hbm.at[mp, g],
            send_sem=ag_send.at[g, s - 1], recv_sem=ag_recv.at[g, s - 1],
            device_id=(me, panel(s)), device_id_type=MESH,
        )

    def out_copies(g):
        return (
            pltpu.make_async_copy(shv.at[g], sh_hbm.at[mp, g], out_sem.at[g, 0]),
            pltpu.make_async_copy(smv.at[g], sm_hbm.at[g], out_sem.at[g, 1]),
        )

    for g in range(groups):
        gather_info(g)
        local_map(g)
        each_peer(lambda s: cm_copy(g, s).start())
    for g in range(groups):
        each_peer(lambda s: cm_copy(g, s).wait_recv())
        finish(g)
        for s in range(1, pn):
            ag_copy(g, s).start()
        for copy in out_copies(g):
            copy.start()
    for g in range(groups):
        for s in range(1, pn):
            rs_copy(g, s).wait_send()
        each_peer(lambda s: cm_copy(g, s).wait_send())
        for copy in out_copies(g):
            copy.wait()
        for s in range(1, pn):
            ag_copy(g, s).wait()


def predict_kernel(pn, groups, gw, tile_group, readout, sh, sm, predicted, smoothed):
    total = None
    for p in range(pn):
        for g in range(groups):
            first = (p * groups + g) * gw
            term = lax.dot_general(
                readout[:, first:first + gw], sh[p, g],
                (((1,), (1,)), ((), ())), preferred_element_type=jnp.float32,
            )
            total = term if total is None else total + term
    predicted[...] = total.astype(jnp.bfloat16)
    smoothed[...] = sm[0].T


def body(observations, info_weight, readout, labels, rate, angle, gain):
    units, bins = observations.shape
    n, pn = lax.axis_size("tm"), lax.axis_size("panel")
    lat = info_weight.shape[1] // pn
    gw = 2 * LANES if lat % (2 * LANES) == 0 else LANES
    groups = lat // gw
    regimes = rate.shape[0]
    steps = bins // CHUNKS

    mag = jnp.exp(-rate)
    spread = -jnp.expm1(-2.0 * rate)
    table = jnp.stack([mag * jnp.cos(angle), mag * jnp.sin(angle), gain * jnp.sqrt(spread), spread])
    table = table.reshape(4 * regimes, groups, gw // 2)
    table = jnp.pad(table, ((0, 0), (0, 0), (0, LANES - gw // 2))).reshape(4 * regimes, groups * LANES)
    lab = jnp.broadcast_to(labels.reshape(CHUNKS, steps).T.reshape(bins, 1), (bins, LANES))

    f32, bf16 = jnp.float32, jnp.bfloat16
    vm = pltpu.VMEM
    dma = pltpu.SemaphoreType.DMA
    big = (groups, bins, LANES)
    peers = max(pn - 1, 1)
    sm, sh = pl.pallas_call(
        functools.partial(smooth_kernel, n, pn, groups, gw, regimes),
        out_shape=(
            jax.ShapeDtypeStruct((groups, bins, gw), f32),
            jax.ShapeDtypeStruct((pn, groups, bins, gw), bf16),
        ),
        in_specs=[pl.BlockSpec(memory_space=pl.ANY)] * 2 + [pl.BlockSpec(memory_space=vm)] * 2,
        out_specs=[pl.BlockSpec(memory_space=pl.ANY)] * 2,
        scratch_shapes=[
            vm((units, bins), bf16),
            vm((bins, units), bf16),
            vm((pn, units, lat), bf16),
            vm((bins, lat), f32),
            vm((groups, peers, bins, gw), bf16),
            vm((groups, peers, bins, gw), bf16),
        ] + [vm(big, f32)] * 9 + [
            vm((groups, 13, CHUNKS, LANES), f32),
            vm((groups, n, ROWS, LANES), f32),
            vm((groups, n, 8, LANES), f32),
            vm((groups, 4, CHUNKS, LANES), f32),
            vm((groups, bins, gw), f32),
            vm((groups, bins, gw), bf16),
            dma((pn + 1,)),
            dma((groups, peers)),
            dma((groups, peers)),
            dma((groups, n)),
            dma((groups, n)),
            dma((groups, peers)),
            dma((groups, peers)),
            dma((groups, 2)),
        ],
        compiler_params=pltpu.CompilerParams(
            collective_id=0, has_side_effects=True, vmem_limit_bytes=36 * 2**20
        ),
        cost_estimate=pl.CostEstimate(
            flops=2 * units * bins * lat * pn, bytes_accessed=2 * units * (bins + lat * pn),
            transcendentals=0,
        ),
        name="smooth",
    )(observations, info_weight, lab, table)

    tiles = lat // LANES
    rows = readout.shape[0] // tiles
    per = gw // LANES
    predicted, smoothed = pl.pallas_call(
        functools.partial(predict_kernel, pn, groups, gw, per),
        grid=(tiles,),
        out_shape=(
            jax.ShapeDtypeStruct((readout.shape[0], bins), bf16),
            jax.ShapeDtypeStruct((lat, bins), f32),
        ),
        in_specs=[
            pl.BlockSpec((rows, lat * pn), lambda i: (i, 0)),
            pl.BlockSpec((pn, groups, bins, gw), lambda i: (0, 0, 0, 0)),
            pl.BlockSpec((1, bins, LANES), lambda i: (i // per, 0, i % per)),
        ],
        out_specs=[
            pl.BlockSpec((rows, bins), lambda i: (i, 0)),
            pl.BlockSpec((LANES, bins), lambda i: (i, 0)),
        ],
        compiler_params=pltpu.CompilerParams(vmem_limit_bytes=24 * 2**20),
        cost_estimate=pl.CostEstimate(
            flops=2 * readout.shape[0] * bins * lat * pn,
            bytes_accessed=2 * readout.shape[0] * (lat * pn + bins) + 8 * bins * lat,
            transcendentals=0,
        ),
        name="predict",
    )(readout, sh, sm)
    return (smoothed, predicted)


def solution(mesh):
    return jax.shard_map(
        body,
        mesh=mesh,
        in_specs=(
            P("panel", "tm"),
            P("panel", None),
            P("panel", None),
            P("tm"),
            P(None, "panel"),
            P(None, "panel"),
            P(None, "panel"),
        ),
        out_specs=(P("panel", "tm"), P("panel", "tm")),
        check_vma=False,
    )
```

time: 1570 us -> 46.7 us (0.03)
  local copies, waits for them, and re-layouts: 1120 us -> 4.85 us
  blocking collectives: 241 us -> 0 us
  other arithmetic: 131 us -> 0.78 us
  Pallas kernels: 0 us -> 40.2 us
  waiting for transfers between devices: 27.1 us -> 0 us
  between operations: 18 us -> 0.68 us
    slice x217 -> x0, local copies, waits for them, and re-layouts: 644 us -> none  [the longest x110 330 us: body(): lax.associative_scan(compose, (gre, gim, coef * mre, coef * mim), reverse...]
    pad x128 -> x0, local copies, waits for them, and re-layouts: 338 us -> none  [the longest x64 178 us: body(): lax.associative_scan(compose, (gre, gim, coef * mre, coef * mim), reverse...]
    all_gather x8 -> x0, blocking collectives: 241 us -> none  [entering(): pieces = jax.tree.map(lambda part: lax.all_gather(part, axis), value)]
    add x121 -> x0, other arithmetic: 66.8 us -> none  [the longest x40 30.3 us: body(): lax.associative_scan(compose, (gre, gim, coef * mre, coef * mim), reverse...]
    mul x48 -> x0, local copies, waits for them, and re-layouts: 47.2 us -> none  [the longest x6 6.52 us: compose(): lim * ebr]
    pallas_call x0 -> x2, Pallas kernels: none -> 40.2 us  [the longest x1 36.1 us: body(): pl.pallas_call(functools.partial(smooth_kernel, n, pn, groups, gw, regime...]
    unnamed x282 -> x6, local copies, waits for them, and re-layouts: 43.3 us -> 3.78 us
    all_gather x2 -> x0, waiting for transfers between devices: 24.8 us -> none  [the longest x1 24.8 us: body(): lax.all_gather(smoothed_half, 'panel', axis=0, tiled=True)]
  transfers between devices with their start and end apart: 4 -> 0, of which waited for: 2 -> 0; matrix products, arithmetic and copies ran while one was open for 12% -> 0% of each run, Pallas kernels for 0% -> 0%
where the time goes in v1:
time: 46.7 us; the launch traced here: 46.5 us
  Pallas kernels  40.2 us (86%)
  local copies, waits for them, and re-layouts  4.85 us (10%)
  other arithmetic  0.78 us (2%)
  between operations  0.68 us (1%)
    pallas_call x1, Pallas kernels, body(): pl.pallas_call(functools.partial(smooth_kernel, n, pn, groups, gw, regime...  36.1 us
    pallas_call x1, Pallas kernels, body(): pl.pallas_call(functools.partial(predict_kernel, pn, groups, gw, per), gr...  4.09 us
    unnamed x6, local copies, waits for them, and re-layouts  3.78 us

profile of v1, /device:TPU:0, one launch (start us, length us, event | category | flops | bytes accessed | tf_op | source)
XLA Modules:
  0.0 46.5 jit_solution(11567494892172120035)
XLA Ops:
  0.6 0.8 %reshape.14 = s32[8,64]{1,0:T(8,128)S(1)} reshape(s32[512]{0:T(512)} %param.10) | data formatting | bytes 4096 | tf_op jit(solution)/shard_map/reshape | solution.py:355
  1.4 0.8 %multiply_bitcast_fusion.2 = (f32[1,4,256]{2,1,0:T(4,128)S(1)}, f32[1,4,256]{2,1,0:T(4,128)S(1)}, f32[1,4,256]{2,1,0:T(4,128)S(1)}, f32[1,4,256]{2,1,0:T(4,128)S(1)}) fusion(f32[4,256]{1,0:T(4,128)} %param.12, f32[4,256]{1,0:T(4,128)} %param.11, f32[4,256]{1,0:T(4,128)} %param.13), kind=kLoop, calls=%fused_computation.4 | loop fusion | flops 6144 | bytes 28672 | tf_op jit(solution)/shard_map/stack | solution.py:352
  2.2 0.1 copy.9
  2.3 0.1 broadcast_in_dim.7
  2.4 0.1 broadcast_in_dim.8.lab_ref
  2.5 0.0 copy-start
  2.5 2.2 %copy-done = bf16[2048,1024]{1,0:T(8,128)(2,1)S(1)} copy-done((bf16[2048,1024]{1,0:T(8,128)(2,1)S(1)}, bf16[2048,1024]{1,0:T(8,128)(2,1)}, u32[]{:S(2)}) %copy-start) | copy-done | bytes 4194328
  4.7 0.0 copy-start.2
  4.7 1.6 %copy-done.2 = bf16[2048,512]{1,0:T(8,128)(2,1)S(1)} copy-done((bf16[2048,512]{1,0:T(8,128)(2,1)S(1)}, bf16[2048,512]{1,0:T(8,128)(2,1)}, u32[]{:S(2)}) %copy-start.2) | copy-done | bytes 2097176
  6.3 0.0 copy-start.1
  6.3 36.1 %smooth.1 = (f32[2,512,256]{2,1,0:T(8,128)S(1)}, bf16[2,2,512,256]{3,2,1,0:T(8,128)(2,1)S(1)}) custom-call(bf16[2048,512]{1,0:T(8,128)(2,1)S(1)} %copy-done.2, bf16[2048,1024]{1,0:T(8,128)(2,1)S(1)} %copy-done, s32[512,128]{1,0:T(8,128)S(1)} %broadcast_in_dim.8.lab_ref, f32[16,256]{1,0:T(8,128)S(1)} %reshape.15.tab_ref), custom_call_target="tpu_custom_call" | custom-call | flops 2147483648 | bytes 6291456 | tf_op jit(solution)/shard_map/smooth/pallas_call | solution.py:362
  42.4 0.0 copy-done.1
  42.4 4.1 %predict.1 = (bf16[2048,512]{1,0:T(8,128)(2,1)}, f32[512,512]{1,0:T(8,128)}) custom-call(bf16[2048,1024]{1,0:T(8,128)(2,1)S(1)} %copy-done.1, bf16[2,2,512,256]{3,2,1,0:T(8,128)(2,1)S(1)} %get-tuple-element.6.sh, f32[2,512,256]{2,1,0:T(8,128)S(1)} %get-tuple-element.7.sm), custom_call_target="tpu_custom_call" | custom-call | flops 2147483648 | bytes 8388608 | tf_op jit(solution)/shard_map/predict/pallas_call | solution.py:406
  (2 shorter events, 0.0 us)
Async XLA Ops:
  2.5 2.2 %copy-start = (bf16[2048,1024]{1,0:T(8,128)(2,1)S(1)}, bf16[2048,1024]{1,0:T(8,128)(2,1)}, u32[]{:S(2)}) copy-start(bf16[2048,1024]{1,0:T(8,128)(2,1)} %w_hbm.1) | copy-start | bytes 12582916
  4.7 1.6 %copy-start.2 = (bf16[2048,512]{1,0:T(8,128)(2,1)S(1)}, bf16[2048,512]{1,0:T(8,128)(2,1)}, u32[]{:S(2)}) copy-start(bf16[2048,512]{1,0:T(8,128)(2,1)} %obs_hbm.1) | copy-start | bytes 6291460
  6.3 36.1 %copy-start.1 = (bf16[2048,1024]{1,0:T(8,128)(2,1)S(1)}, bf16[2048,1024]{1,0:T(8,128)(2,1)}, u32[]{:S(2)}) copy-start(bf16[2048,1024]{1,0:T(8,128)(2,1)} %readout.1) | copy-start | bytes 12582916

commit v2 on v1

--- a/solution.py
+++ b/solution.py
@@ -28,11 +28,11 @@
 
 def smooth_kernel(
     n, pn, groups, gw, regimes,
-    obs_hbm, w_hbm, lab_ref, tab_ref,
+    obs_hbm, w_hbm, lab_hbm, rate_hbm, angle_hbm, gain_hbm,
     sm_hbm, sh_hbm,
-    obs, obs_t, w, own, rs_out, rs_in, xre, xim, are, aim, coef, mre, mim, pre, pim,
-    chunk, msgs, enter, bound, smv, shv,
-    in_sem, rs_send, rs_recv, cm_send, cm_recv, ag_send, ag_recv, out_sem,
+    obs, obs_t, w, own, rs_out, rs_in, xre, xim, are, aim, scl, vre, vim, coef, mre, mim, pre, pim,
+    lab_ref, rate_ref, angle_ref, gain_ref, lab, lab_rows, chunk, msgs, enter, bound, smv, shv,
+    in_sem, small_sem, rs_send, rs_recv, cm_send, cm_recv, ag_send, ag_recv, out_sem,
 ):
     me = lax.axis_index("tm")
     mp = lax.axis_index("panel")
@@ -52,6 +52,15 @@
         w_copies[s] = pltpu.make_async_copy(w_hbm.at[:, columns], w.at[s], in_sem.at[1 + s])
         w_copies[s].start()
 
+    small_copies = [
+        pltpu.make_async_copy(src, dst, small_sem.at[i])
+        for i, (src, dst) in enumerate((
+            (lab_hbm, lab_ref), (rate_hbm, rate_ref), (angle_hbm, angle_ref), (gain_hbm, gain_ref)
+        ))
+    ]
+    for copy in small_copies:
+        copy.start()
+
     barrier = pltpu.get_barrier_semaphore()
 
     for s in range(1, pn):
@@ -64,6 +73,75 @@
         return 0
 
     lax.fori_loop(1, n, greet, 0)
+
+    def rows_of(k):
+        return pl.ds(pl.multiple_of(k * CHUNKS, CHUNKS), CHUNKS)
+
+    def spread_labels():
+        for c in range(CHUNKS):
+            row, first = divmod(c * steps, LANES)
+            x = lab_ref[row:row + 1, :]
+            lab_rows[c:c + 1, :] = x if first == 0 else pltpu.roll(x, LANES - first, 1)
+        x = lab_rows[...]
+        for k in range(steps):
+            lab[k * CHUNKS:(k + 1) * CHUNKS, :] = jnp.broadcast_to(x[:, k:k + 1], (CHUNKS, LANES))
+
+    def prepare(g):
+        lanes = slice(g * LANES, (g + 1) * LANES)
+        rate, angle = rate_ref[:, lanes], angle_ref[:, lanes]
+        x = 2.0 * rate
+        series = 1.0 - x * (1.0 / 8.0)
+        for term in range(7, 1, -1):
+            series = 1.0 - x * (1.0 / term) * series
+        spread = jnp.where(x < 0.25, x * series, 1.0 - jnp.exp(-x))
+        mag = jnp.exp(-rate)
+        values = (
+            mag * jnp.cos(angle), mag * jnp.sin(angle),
+            gain_ref[:, lanes] * jnp.sqrt(spread), spread,
+        )
+        table = [
+            [jnp.broadcast_to(v[r:r + 1, :], (CHUNKS, LANES)) for r in range(regimes)]
+            for v in values
+        ]
+
+        def at(k):
+            label = lab[rows_of(k), :]
+            which = [label == r for r in range(regimes)]
+
+            def pick(q):
+                value = table[q][0]
+                for r in range(1, regimes):
+                    value = jnp.where(which[r], table[q][r], value)
+                return value
+
+            return (pick(0), pick(1)), pick(2), pick(3)
+
+        def keep(k, a, scale, c, p):
+            rows = rows_of(k)
+            are[g, rows, :], aim[g, rows, :] = a
+            scl[g, rows, :], coef[g, rows, :] = scale, c
+            pre[g, rows, :], pim[g, rows, :] = p
+
+        def step(k, carry):
+            p, q, d = carry
+            a, scale, c = at(k)
+            v = (c * q[0], -(c * q[1]))
+            before = rows_of(k - 1)
+            vre[g, before, :], vim[g, before, :] = v
+            d = add(d, mul(v, p))
+            p, q = mul(a, p), mul(a, q)
+            keep(k, a, scale, c, p)
+            return p, q, d
+
+        zero = jnp.zeros((CHUNKS, LANES), jnp.float32)
+        one = jnp.ones((CHUNKS, LANES), jnp.float32)
+        a0, scale0, c0 = at(0)
+        keep(0, a0, scale0, c0, a0)
+        p, q, d = lax.fori_loop(1, steps, step, (a0, (one, zero), (zero, zero)), unroll=3)
+        end = rows_of(steps - 1)
+        vre[g, end, :], vim[g, end, :] = zero, zero
+        for row, x in zip((0, 1, 4, 5, 8, 9, 10, 11, 12), (*p, q[0], -q[1], *d, *a0, c0)):
+            chunk[g, row] = x
 
     obs_copy.wait()
     tile = 256
@@ -98,6 +176,12 @@
     w_copies[0].wait()
     for g in range(groups):
         own[:, g * gw:(g + 1) * gw] = project(g, 0)
+
+    for copy in small_copies:
+        copy.wait()
+    spread_labels()
+    for g in range(groups):
+        prepare(g)
 
     lane = lax.broadcasted_iota(jnp.int32, (bins, LANES), 1)
     low = lane < HALF
@@ -121,61 +205,22 @@
             xre[g] = parts[0]
             xim[g] = swap(parts[0])
 
-    def rows_of(k):
-        return pl.ds(pl.multiple_of(k * CHUNKS, CHUNKS), CHUNKS)
-
-    def forward(g):
-        def row(q, r):
-            return jnp.broadcast_to(
-                tab_ref[q * regimes + r:q * regimes + r + 1, g * LANES:(g + 1) * LANES],
-                (CHUNKS, LANES),
-            )
-
-        table = [[row(q, r) for r in range(regimes)] for q in range(4)]
-
+    def scan(g):
         def step(k, carry):
-            m, p = carry
+            m, e = carry
             rows = rows_of(k)
-            label = lab_ref[rows, :]
-            which = [label == r for r in range(regimes)]
-
-            def pick(q):
-                value = table[q][0]
-                for r in range(1, regimes):
-                    value = jnp.where(which[r], table[q][r], value)
-                return value
-
-            a = (pick(0), pick(1))
-            scale, c = pick(2), pick(3)
             bin_rows = pl.ds(k, CHUNKS, stride=steps)
+            scale = scl[g, rows, :]
             u = (scale * xre[g, bin_rows, :], scale * xim[g, bin_rows, :])
-            m = add(mul(a, m), u)
-            p = mul(a, p)
-            are[g, rows, :], aim[g, rows, :], coef[g, rows, :] = a[0], a[1], c
+            m = add(mul((are[g, rows, :], aim[g, rows, :]), m), u)
+            e = add(e, mul((vre[g, rows, :], vim[g, rows, :]), m))
             mre[g, rows, :], mim[g, rows, :] = m
-            pre[g, rows, :], pim[g, rows, :] = p
-            return m, p
+            return m, e
 
         zero = jnp.zeros((CHUNKS, LANES), jnp.float32)
-        one = jnp.ones((CHUNKS, LANES), jnp.float32)
-        return lax.fori_loop(0, steps, step, ((zero, zero), (one, zero)), unroll=4)
-
-    def backward(g):
-        def step(i, carry):
-            e, d, w_ = carry
-            k = steps - 2 - i
-            rows, after = rows_of(k), rows_of(k + 1)
-            a = (are[g, after, :], aim[g, after, :])
-            c = coef[g, after, :]
-            e = add(cmul(a, e), (c * mre[g, rows, :], c * mim[g, rows, :]))
-            d = add(cmul(a, d), (c * pre[g, rows, :], c * pim[g, rows, :]))
-            return e, d, cmul(a, w_)
-
-        zero = jnp.zeros((CHUNKS, LANES), jnp.float32)
-        one = jnp.ones((CHUNKS, LANES), jnp.float32)
-        return lax.fori_loop(
-            0, steps - 1, step, ((zero, zero), (zero, zero), (one, zero)), unroll=3
-        )
+        b, e = lax.fori_loop(0, steps, step, ((zero, zero), (zero, zero)), unroll=4)
+        chunk[g, 2], chunk[g, 3] = b
+        chunk[g, 6], chunk[g, 7] = e
 
     def chunk_row(g, q, c):
         return chunk[g, q, c:c + 1, :]
@@ -185,12 +230,7 @@
         return (v[0], v[1]), (v[2], v[3]), (v[4], v[5]), (v[6], v[7]), (v[8], v[9]), (v[10], v[11]), v[12]
 
     def local_map(g):
-        b, a = forward(g)
-        e, d, w_ = backward(g)
-        first = rows_of(0)
-        parts = (*a, *b, *w_, *e, *d, are[g, first, :], aim[g, first, :], coef[g, first, :])
-        for q in range(13):
-            chunk[g, q] = parts[q]
+        scan(g)
         A, B, G, E, D, a0, c0 = chunk_map(g, 0)
         for c in range(1, CHUNKS):
             Ar, Br, Gr, Er, Dr, ar, cr = chunk_map(g, c)
@@ -236,7 +276,7 @@
             put(d, 0, m)
             return add(mul(pair(slot, 0), m), pair(slot, 2))
 
-        last = lax.fori_loop(0, n, ahead, (zero, zero))
+        last = lax.fori_loop(0, n, ahead, (zero, zero), unroll=4)
 
         def back(i, s):
             d = n - 1 - i
@@ -247,7 +287,7 @@
             c = msgs[g, slot, 12:13, :]
             return add(cmul(pair(slot, 10), first), (c * m[0], c * m[1]))
 
-        lax.fori_loop(0, n, back, last)
+        lax.fori_loop(0, n, back, last, unroll=4)
         m_in, s_in = get(me, 0), get(me, 2)
         return m_in, s_in
 
@@ -290,16 +330,19 @@
             smv[g, :, h * LANES:(h + 1) * LANES] = x
             shv[g, :, h * LANES:(h + 1) * LANES] = x.astype(jnp.bfloat16)
 
+    def sh_columns(g):
+        return pl.ds(pl.multiple_of(mp * lat + g * gw, LANES), gw)
+
     def ag_copy(g, s):
         return pltpu.make_async_remote_copy(
-            src_ref=shv.at[g], dst_ref=sh_hbm.at[mp, g],
+            src_ref=shv.at[g], dst_ref=sh_hbm.at[:, sh_columns(g)],
             send_sem=ag_send.at[g, s - 1], recv_sem=ag_recv.at[g, s - 1],
             device_id=(me, panel(s)), device_id_type=MESH,
         )
 
     def out_copies(g):
         return (
-            pltpu.make_async_copy(shv.at[g], sh_hbm.at[mp, g], out_sem.at[g, 0]),
+            pltpu.make_async_copy(shv.at[g], sh_hbm.at[:, sh_columns(g)], out_sem.at[g, 0]),
             pltpu.make_async_copy(smv.at[g], sm_hbm.at[g], out_sem.at[g, 1]),
         )
 
@@ -307,7 +350,6 @@
         gather_info(g)
         local_map(g)
         each_peer(lambda s: cm_copy(g, s).start())
-    for g in range(groups):
         each_peer(lambda s: cm_copy(g, s).wait_recv())
         finish(g)
         for s in range(1, pn):
@@ -324,18 +366,49 @@
             ag_copy(g, s).wait()
 
 
-def predict_kernel(pn, groups, gw, tile_group, readout, sh, sm, predicted, smoothed):
-    total = None
-    for p in range(pn):
-        for g in range(groups):
-            first = (p * groups + g) * gw
-            term = lax.dot_general(
-                readout[:, first:first + gw], sh[p, g],
-                (((1,), (1,)), ((), ())), preferred_element_type=jnp.float32,
-            )
-            total = term if total is None else total + term
-    predicted[...] = total.astype(jnp.bfloat16)
-    smoothed[...] = sm[0].T
+def predict_kernel(
+    tiles, readout_hbm, sh_hbm, sm_hbm, predicted, smoothed,
+    readout, sh, sm, out, turned, in_sems, sems,
+):
+    rows = readout.shape[0] // tiles
+    per = sm.shape[2] // LANES
+    loads, copies = [], []
+
+    def send(src, dst):
+        copy = pltpu.make_async_copy(src, dst, sems.at[len(copies)])
+        copy.start()
+        copies.append(copy)
+
+    def fetch(src, dst):
+        load = pltpu.make_async_copy(src, dst, in_sems.at[len(loads)])
+        load.start()
+        loads.append(load)
+
+    fetch(sh_hbm, sh)
+    for i in range(tiles):
+        part = pl.ds(i * rows, rows)
+        fetch(readout_hbm.at[part], readout.at[part])
+        if i == 0:
+            fetch(sm_hbm, sm)
+    sh_load, first, sm_load, *later = loads
+    loads = [first, *later]
+    sh_load.wait()
+    for i in range(tiles):
+        lanes = slice(i * LANES, (i + 1) * LANES)
+        here = slice((i % per) * LANES, (i % per + 1) * LANES)
+        part = pl.ds(i * rows, rows)
+        loads[i].wait()
+        out[part, :] = lax.dot_general(
+            readout[part, :], sh[...],
+            (((1,), (1,)), ((), ())), preferred_element_type=jnp.float32,
+        ).astype(jnp.bfloat16)
+        send(out.at[part], predicted.at[part])
+        if i == 0:
+            sm_load.wait()
+        turned[lanes, :] = sm[i // per, :, here].T
+        send(turned.at[pl.ds(i * LANES, LANES)], smoothed.at[pl.ds(i * LANES, LANES)])
+    for copy in copies:
+        copy.wait()
 
 
 def body(observations, info_weight, readout, labels, rate, angle, gain):
@@ -345,14 +418,13 @@
     gw = 2 * LANES if lat % (2 * LANES) == 0 else LANES
     groups = lat // gw
     regimes = rate.shape[0]
-    steps = bins // CHUNKS
-
-    mag = jnp.exp(-rate)
-    spread = -jnp.expm1(-2.0 * rate)
-    table = jnp.stack([mag * jnp.cos(angle), mag * jnp.sin(angle), gain * jnp.sqrt(spread), spread])
-    table = table.reshape(4 * regimes, groups, gw // 2)
-    table = jnp.pad(table, ((0, 0), (0, 0), (0, LANES - gw // 2))).reshape(4 * regimes, groups * LANES)
-    lab = jnp.broadcast_to(labels.reshape(CHUNKS, steps).T.reshape(bins, 1), (bins, LANES))
+
+    short = groups * LANES - rate.shape[1]
+    if short:
+        rate, angle, gain = (
+            jnp.pad(x, ((0, 0), (0, short)), constant_values=0.25) for x in (rate, angle, gain)
+        )
+    lab = labels.reshape(bins // LANES, LANES)
 
     f32, bf16 = jnp.float32, jnp.bfloat16
     vm = pltpu.VMEM
@@ -363,9 +435,9 @@
         functools.partial(smooth_kernel, n, pn, groups, gw, regimes),
         out_shape=(
             jax.ShapeDtypeStruct((groups, bins, gw), f32),
-            jax.ShapeDtypeStruct((pn, groups, bins, gw), bf16),
+            jax.ShapeDtypeStruct((bins, pn * lat), bf16),
         ),
-        in_specs=[pl.BlockSpec(memory_space=pl.ANY)] * 2 + [pl.BlockSpec(memory_space=vm)] * 2,
+        in_specs=[pl.BlockSpec(memory_space=pl.ANY)] * 6,
         out_specs=[pl.BlockSpec(memory_space=pl.ANY)] * 2,
         scratch_shapes=[
             vm((units, bins), bf16),
@@ -374,7 +446,11 @@
             vm((bins, lat), f32),
             vm((groups, peers, bins, gw), bf16),
             vm((groups, peers, bins, gw), bf16),
-        ] + [vm(big, f32)] * 9 + [
+        ] + [vm(big, f32)] * 12 + [
+            vm((bins // LANES, LANES), jnp.int32),
+        ] + [vm(rate.shape, f32)] * 3 + [
+            vm((bins, LANES), jnp.int32),
+            vm((CHUNKS, LANES), jnp.int32),
             vm((groups, 13, CHUNKS, LANES), f32),
             vm((groups, n, ROWS, LANES), f32),
             vm((groups, n, 8, LANES), f32),
@@ -382,6 +458,7 @@
             vm((groups, bins, gw), f32),
             vm((groups, bins, gw), bf16),
             dma((pn + 1,)),
+            dma((4,)),
             dma((groups, peers)),
             dma((groups, peers)),
             dma((groups, n)),
@@ -391,35 +468,34 @@
             dma((groups, 2)),
         ],
         compiler_params=pltpu.CompilerParams(
-            collective_id=0, has_side_effects=True, vmem_limit_bytes=36 * 2**20
+            collective_id=0, has_side_effects=True, vmem_limit_bytes=61 * 2**20
         ),
         cost_estimate=pl.CostEstimate(
             flops=2 * units * bins * lat * pn, bytes_accessed=2 * units * (bins + lat * pn),
             transcendentals=0,
         ),
         name="smooth",
-    )(observations, info_weight, lab, table)
+    )(observations, info_weight, lab, rate, angle, gain)
 
     tiles = lat // LANES
-    rows = readout.shape[0] // tiles
-    per = gw // LANES
     predicted, smoothed = pl.pallas_call(
-        functools.partial(predict_kernel, pn, groups, gw, per),
-        grid=(tiles,),
+        functools.partial(predict_kernel, tiles),
         out_shape=(
             jax.ShapeDtypeStruct((readout.shape[0], bins), bf16),
             jax.ShapeDtypeStruct((lat, bins), f32),
         ),
-        in_specs=[
-            pl.BlockSpec((rows, lat * pn), lambda i: (i, 0)),
-            pl.BlockSpec((pn, groups, bins, gw), lambda i: (0, 0, 0, 0)),
-            pl.BlockSpec((1, bins, LANES), lambda i: (i // per, 0, i % per)),
+        in_specs=[pl.BlockSpec(memory_space=pl.ANY)] * 3,
+        out_specs=[pl.BlockSpec(memory_space=pltpu.HBM)] * 2,
+        scratch_shapes=[
+            vm(readout.shape, bf16),
+            vm(sh.shape, bf16),
+            vm(sm.shape, f32),
+            vm((readout.shape[0], bins), bf16),
+            vm((lat, bins), f32),
+            dma((tiles + 2,)),
+            dma((2 * tiles,)),
         ],
-        out_specs=[
-            pl.BlockSpec((rows, bins), lambda i: (i, 0)),
-            pl.BlockSpec((LANES, bins), lambda i: (i, 0)),
-        ],
-        compiler_params=pltpu.CompilerParams(vmem_limit_bytes=24 * 2**20),
+        compiler_params=pltpu.CompilerParams(vmem_limit_bytes=61 * 2**20),
         cost_estimate=pl.CostEstimate(
             flops=2 * readout.shape[0] * bins * lat * pn,
             bytes_accessed=2 * readout.shape[0] * (lat * pn + bins) + 8 * bins * lat,

time: 46.7 us -> 42.6 us (0.912)
  local copies, waits for them, and re-layouts: 4.85 us -> 0 us
  Pallas kernels: 40.2 us -> 41.8 us
  other arithmetic: 0.78 us -> 0 us
    unnamed x6 -> x0, local copies, waits for them, and re-layouts: 3.78 us -> none
    pallas_call x1, Pallas kernels: 4.09 us -> 5.66 us  [body(): pl.pallas_call(functools.partial(predict_kernel, tiles), out_shape=(jax.S...]
    another operation x2 -> x0, other arithmetic: 0.78 us -> none  [body(): jnp.stack([mag * jnp.cos(angle), mag * jnp.sin(angle), gain * jnp.sqrt(sp...]
    reshape x2 -> x0, local copies, waits for them, and re-layouts: 0.77 us -> none  [the longest x1 0.76 us: body(): labels.reshape(CHUNKS, steps).T.reshape(bins, 1)]
where the time goes in v2:
time: 42.6 us; the launch traced here: 42.5 us
  Pallas kernels  41.8 us (98%)
  between operations  0.64 us (2%)
    pallas_call x1, Pallas kernels, body(): pl.pallas_call(functools.partial(smooth_kernel, n, pn, groups, gw, regime...  36.2 us
    pallas_call x1, Pallas kernels, body(): pl.pallas_call(functools.partial(predict_kernel, tiles), out_shape=(jax.S...  5.66 us

profile of v2, /device:TPU:0, one launch (start us, length us, event | category | flops | bytes accessed | tf_op | source)
XLA Modules:
  0.0 42.5 jit_solution(6618961661481713824)
XLA Ops:
  0.6 36.2 %smooth.1 = (f32[2,512,256]{2,1,0:T(8,128)}, bf16[512,1024]{1,0:T(8,128)(2,1)}) custom-call(bf16[2048,512]{1,0:T(8,128)(2,1)} %obs_hbm.1, bf16[2048,1024]{1,0:T(8,128)(2,1)} %w_hbm.1, s32[4,128]{1,0:T(4,128)} %bitcast.1, f32[4,256]{1,0:T(4,128)} %rate_hbm.1, f32[4,256]{1,0:T(4,128)} %angle_hbm.1, f32[4,256]{1,0:T(4,128)} %gain_hbm.1), custom_call_target="tpu_custom_call" | custom-call | flops 2147483648 | bytes 6291456 | tf_op jit(solution)/shard_map/smooth/pallas_call | solution.py:434
  36.8 5.7 %predict.1 = (bf16[2048,512]{1,0:T(8,128)(2,1)}, f32[512,512]{1,0:T(8,128)}) custom-call(bf16[2048,1024]{1,0:T(8,128)(2,1)} %readout_hbm.1, bf16[512,1024]{1,0:T(8,128)(2,1)} %get-tuple-element.6.sh_hbm, f32[2,512,256]{2,1,0:T(8,128)} %get-tuple-element.7.sm_hbm), custom_call_target="tpu_custom_call" | custom-call | flops 2147483648 | bytes 8388608 | tf_op jit(solution)/shard_map/predict/pallas_call | solution.py:481

commit v3 on v2

--- a/solution.py
+++ b/solution.py
@@ -10,7 +10,8 @@
 LANES = 128
 HALF = 64
 CHUNKS = 8
-ROWS = 16
+TURN = 256
+FIXED = 9
 MESH = pl.DeviceIdType.MESH
 
 
@@ -31,8 +32,8 @@
     obs_hbm, w_hbm, lab_hbm, rate_hbm, angle_hbm, gain_hbm,
     sm_hbm, sh_hbm,
     obs, obs_t, w, own, rs_out, rs_in, xre, xim, are, aim, scl, vre, vim, coef, mre, mim, pre, pim,
-    lab_ref, rate_ref, angle_ref, gain_ref, lab, lab_rows, chunk, msgs, enter, bound, smv, shv,
-    in_sem, small_sem, rs_send, rs_recv, cm_send, cm_recv, ag_send, ag_recv, out_sem,
+    lab_ref, rate_ref, angle_ref, gain_ref, lab, lab_rows, chunk, joint, fixed, moving, enter, bound, smv, smt, shv,
+    obs_sem, w_sem, small_sem, rs_send, rs_recv, fx_send, fx_recv, cm_send, cm_recv, ag_send, ag_recv, out_sem,
 ):
     me = lax.axis_index("tm")
     mp = lax.axis_index("panel")
@@ -44,13 +45,26 @@
     def panel(s):
         return lax.rem(mp + s, pn)
 
-    obs_copy = pltpu.make_async_copy(obs_hbm, obs, in_sem.at[0])
-    obs_copy.start()
-    w_copies = {}
-    for s in list(range(1, pn)) + [0]:
-        columns = pl.ds(pl.multiple_of(panel(s) * lat, LANES), lat)
-        w_copies[s] = pltpu.make_async_copy(w_hbm.at[:, columns], w.at[s], in_sem.at[1 + s])
-        w_copies[s].start()
+    turns = units // TURN
+
+    def obs_copy(i):
+        rows = pl.ds(pl.multiple_of(i * TURN, TURN), TURN)
+        return pltpu.make_async_copy(obs_hbm.at[rows], obs.at[rows], obs_sem.at[i])
+
+    def w_copy(g, s):
+        columns = pl.ds(pl.multiple_of(panel(s) * lat + g * gw, LANES), gw)
+        return pltpu.make_async_copy(w_hbm.at[:, columns], w.at[s, g], w_sem.at[s, g])
+
+    def load(i, _):
+        obs_copy(i).start()
+        return 0
+
+    lax.fori_loop(0, turns, load, 0)
+    for g in range(groups):
+        for s in range(1, pn):
+            w_copy(g, s).start()
+    for g in range(groups):
+        w_copy(g, 0).start()
 
     small_copies = [
         pltpu.make_async_copy(src, dst, small_sem.at[i])
@@ -143,15 +157,40 @@
         for row, x in zip((0, 1, 4, 5, 8, 9, 10, 11, 12), (*p, q[0], -q[1], *d, *a0, c0)):
             chunk[g, row] = x
 
-    obs_copy.wait()
-    tile = 256
+    def chunk_row(g, q, c):
+        return chunk[g, q, c:c + 1, :]
+
+    def pair_row(g, q, c):
+        return chunk_row(g, q, c), chunk_row(g, q + 1, c)
+
+    def chunk_map(g, c):
+        return *(pair_row(g, q, c) for q in (0, 4, 8, 10)), chunk_row(g, 12, c)
+
+    def join_fixed(g):
+        A, G, D, a0, c0 = chunk_map(g, 0)
+        for c in range(1, CHUNKS):
+            Ar, Gr, Dr, ar, cr = chunk_map(g, c)
+            K = cmul(ar, Dr)
+            K = mul(G, (K[0] + cr, K[1]))
+            M = mul(G, (ar[0], -ar[1]))
+            for row, x in enumerate((*M, *K)):
+                joint[g, row, c:c + 1, :] = x
+            D = add(D, mul(K, A))
+            G = mul(M, Gr)
+            A = mul(Ar, A)
+        for row, x in enumerate((*A, *G, *D, *a0, c0)):
+            fixed[0, g * FIXED + row:g * FIXED + row + 1, :] = x
+        last = groups * FIXED
+        if g == groups - 1 and last < fixed.shape[1]:
+            fixed[0, last:, :] = jnp.zeros((fixed.shape[1] - last, LANES), jnp.float32)
 
     def turn(i, _):
-        rows = pl.ds(pl.multiple_of(i * tile, tile), tile)
+        obs_copy(i).wait()
+        rows = pl.ds(pl.multiple_of(i * TURN, TURN), TURN)
         obs_t[:, rows] = obs[rows, :].T
         return 0
 
-    lax.fori_loop(0, units // tile, turn, 0)
+    lax.fori_loop(0, turns, turn, 0)
 
     def rs_copy(g, s):
         return pltpu.make_async_remote_copy(
@@ -161,27 +200,39 @@
         )
 
     def project(g, s):
-        return jnp.dot(
-            obs_t[...], w[s, :, g * gw:(g + 1) * gw], preferred_element_type=jnp.float32
-        )
-
-    for s in range(1, pn):
-        w_copies[s].wait()
+        w_copy(g, s).wait()
+        return jnp.dot(obs_t[...], w[s, g], preferred_element_type=jnp.float32)
+
     for g in range(groups):
         for s in range(1, pn):
             rs_out[g, s - 1] = project(g, s).astype(jnp.bfloat16)
             if g == 0 and s == 1:
                 pl.semaphore_wait(barrier, n - 1 + pn - 1)
             rs_copy(g, s).start()
-    w_copies[0].wait()
-    for g in range(groups):
-        own[:, g * gw:(g + 1) * gw] = project(g, 0)
+
+    def each_peer(act):
+        def go(s, _):
+            act(s)
+            return 0
+
+        lax.fori_loop(1, n, go, 0)
+
+    def fx_copy(s):
+        return pltpu.make_async_remote_copy(
+            src_ref=fixed.at[0], dst_ref=fixed.at[s],
+            send_sem=fx_send.at[s], recv_sem=fx_recv.at[s],
+            device_id=(lax.rem(me + s, n), mp), device_id_type=MESH,
+        )
 
     for copy in small_copies:
         copy.wait()
     spread_labels()
     for g in range(groups):
         prepare(g)
+        join_fixed(g)
+    each_peer(lambda s: fx_copy(s).start())
+    for g in range(groups):
+        own[:, g * gw:(g + 1) * gw] = project(g, 0)
 
     lane = lax.broadcasted_iota(jnp.int32, (bins, LANES), 1)
     low = lane < HALF
@@ -222,48 +273,33 @@
         chunk[g, 2], chunk[g, 3] = b
         chunk[g, 6], chunk[g, 7] = e
 
-    def chunk_row(g, q, c):
-        return chunk[g, q, c:c + 1, :]
-
-    def chunk_map(g, c):
-        v = [chunk_row(g, q, c) for q in range(13)]
-        return (v[0], v[1]), (v[2], v[3]), (v[4], v[5]), (v[6], v[7]), (v[8], v[9]), (v[10], v[11]), v[12]
-
     def local_map(g):
         scan(g)
-        A, B, G, E, D, a0, c0 = chunk_map(g, 0)
+        B, E = pair_row(g, 2, 0), pair_row(g, 6, 0)
         for c in range(1, CHUNKS):
-            Ar, Br, Gr, Er, Dr, ar, cr = chunk_map(g, c)
-            K = cmul(ar, Dr)
-            K = (K[0] + cr, K[1])
-            E = add(E, mul(G, add(cmul(ar, Er), mul(K, B))))
-            D = add(D, mul(G, mul(K, A)))
-            G = mul(G, cmul(ar, Gr))
-            A, B = mul(Ar, A), add(mul(Ar, B), Br)
-        rows = (*A, *B, *G, *E, *D, *a0, c0)
-        for q in range(13):
-            msgs[g, 0, q:q + 1, :] = rows[q]
-        msgs[g, 0, 13:ROWS, :] = jnp.zeros((ROWS - 13, LANES), jnp.float32)
+            M = (joint[g, 0, c:c + 1, :], joint[g, 1, c:c + 1, :])
+            K = (joint[g, 2, c:c + 1, :], joint[g, 3, c:c + 1, :])
+            E = add(E, add(mul(M, pair_row(g, 6, c)), mul(K, B)))
+            B = add(mul(pair_row(g, 0, c), B), pair_row(g, 2, c))
+        for row, x in enumerate((*B, *E)):
+            moving[g, 0, row:row + 1, :] = x
 
     def cm_copy(g, s):
         return pltpu.make_async_remote_copy(
-            src_ref=msgs.at[g, 0], dst_ref=msgs.at[g, s],
+            src_ref=moving.at[g, 0], dst_ref=moving.at[g, s],
             send_sem=cm_send.at[g, s], recv_sem=cm_recv.at[g, s],
             device_id=(lax.rem(me + s, n), mp), device_id_type=MESH,
         )
 
-    def each_peer(act):
-        def go(s, _):
-            act(s)
-            return 0
-
-        lax.fori_loop(1, n, go, 0)
-
     def boundary(g):
         zero = jnp.zeros((1, LANES), jnp.float32)
 
-        def pair(slot, q):
-            return msgs[g, slot, q:q + 1, :], msgs[g, slot, q + 1:q + 2, :]
+        def still(slot, q):
+            q = g * FIXED + q
+            return fixed[slot, q:q + 1, :], fixed[slot, q + 1:q + 2, :]
+
+        def fresh(slot, q):
+            return moving[g, slot, q:q + 1, :], moving[g, slot, q + 1:q + 2, :]
 
         def put(d, row, value):
             enter[g, d, row:row + 1, :], enter[g, d, row + 1:row + 2, :] = value
@@ -274,7 +310,7 @@
         def ahead(d, m):
             slot = lax.rem(me - d + n, n)
             put(d, 0, m)
-            return add(mul(pair(slot, 0), m), pair(slot, 2))
+            return add(mul(still(slot, 0), m), fresh(slot, 0))
 
         last = lax.fori_loop(0, n, ahead, (zero, zero), unroll=4)
 
@@ -283,9 +319,9 @@
             slot = lax.rem(me - d + n, n)
             put(d, 2, s)
             m = get(d, 0)
-            first = add(add(mul(pair(slot, 4), s), pair(slot, 6)), mul(pair(slot, 8), m))
-            c = msgs[g, slot, 12:13, :]
-            return add(cmul(pair(slot, 10), first), (c * m[0], c * m[1]))
+            first = add(add(mul(still(slot, 2), s), fresh(slot, 2)), mul(still(slot, 4), m))
+            c = fixed[slot, g * FIXED + 8:g * FIXED + 9, :]
+            return add(cmul(still(slot, 6), first), (c * m[0], c * m[1]))
 
         lax.fori_loop(0, n, back, last, unroll=4)
         m_in, s_in = get(me, 0), get(me, 2)
@@ -297,13 +333,12 @@
         for c in range(CHUNKS):
             entering.append(m)
             bound[g, 0, c:c + 1, :], bound[g, 1, c:c + 1, :] = m
-            A, B = chunk_map(g, c)[:2]
-            m = add(mul(A, m), B)
+            m = add(mul(pair_row(g, 0, c), m), pair_row(g, 2, c))
         for c in reversed(range(CHUNKS)):
             bound[g, 2, c:c + 1, :], bound[g, 3, c:c + 1, :] = s
-            _, _, G, E, D, a0, c0 = chunk_map(g, c)
+            _, G, D, a0, c0 = chunk_map(g, c)
             m = entering[c]
-            first = add(add(mul(G, s), E), mul(D, m))
+            first = add(add(mul(G, s), pair_row(g, 6, c)), mul(D, m))
             s = add(cmul(a0, first), (c0 * m[0], c0 * m[1]))
         m_in = (bound[g, 0], bound[g, 1])
         s_in = (bound[g, 2], bound[g, 3])
@@ -343,19 +378,30 @@
     def out_copies(g):
         return (
             pltpu.make_async_copy(shv.at[g], sh_hbm.at[:, sh_columns(g)], out_sem.at[g, 0]),
-            pltpu.make_async_copy(smv.at[g], sm_hbm.at[g], out_sem.at[g, 1]),
-        )
+            pltpu.make_async_copy(smt.at[g], sm_hbm.at[pl.ds(g * gw, gw)], out_sem.at[g, 1]),
+        )
+
+    def turn_out(g):
+        for h in range(gw // LANES):
+            lanes = slice(h * LANES, (h + 1) * LANES)
+            smt[g, lanes, :] = smv[g, :, lanes].T
+        out_copies(g)[1].start()
 
     for g in range(groups):
         gather_info(g)
         local_map(g)
         each_peer(lambda s: cm_copy(g, s).start())
+        if g == 0:
+            each_peer(lambda s: fx_copy(s).wait_recv())
+        else:
+            turn_out(g - 1)
         each_peer(lambda s: cm_copy(g, s).wait_recv())
         finish(g)
         for s in range(1, pn):
             ag_copy(g, s).start()
-        for copy in out_copies(g):
-            copy.start()
+        out_copies(g)[0].start()
+    turn_out(groups - 1)
+    each_peer(lambda s: fx_copy(s).wait_send())
     for g in range(groups):
         for s in range(1, pn):
             rs_copy(g, s).wait_send()
@@ -367,46 +413,29 @@
 
 
 def predict_kernel(
-    tiles, readout_hbm, sh_hbm, sm_hbm, predicted, smoothed,
-    readout, sh, sm, out, turned, in_sems, sems,
+    tiles, readout_hbm, sh_hbm, sm_hbm, predicted, smoothed, readout, sh, out, in_sems, sems
 ):
     rows = readout.shape[0] // tiles
-    per = sm.shape[2] // LANES
     loads, copies = [], []
 
-    def send(src, dst):
-        copy = pltpu.make_async_copy(src, dst, sems.at[len(copies)])
-        copy.start()
-        copies.append(copy)
-
-    def fetch(src, dst):
-        load = pltpu.make_async_copy(src, dst, in_sems.at[len(loads)])
-        load.start()
-        loads.append(load)
-
-    fetch(sh_hbm, sh)
+    def begin(into, src, dst, sem):
+        into.append(pltpu.make_async_copy(src, dst, sem))
+        into[-1].start()
+
+    begin(loads, sh_hbm, sh, in_sems.at[tiles])
     for i in range(tiles):
         part = pl.ds(i * rows, rows)
-        fetch(readout_hbm.at[part], readout.at[part])
-        if i == 0:
-            fetch(sm_hbm, sm)
-    sh_load, first, sm_load, *later = loads
-    loads = [first, *later]
-    sh_load.wait()
+        begin(loads, readout_hbm.at[part], readout.at[part], in_sems.at[i])
+    begin(copies, sm_hbm, smoothed, sems.at[tiles])
+    loads[0].wait()
     for i in range(tiles):
-        lanes = slice(i * LANES, (i + 1) * LANES)
-        here = slice((i % per) * LANES, (i % per + 1) * LANES)
         part = pl.ds(i * rows, rows)
-        loads[i].wait()
+        loads[i + 1].wait()
         out[part, :] = lax.dot_general(
             readout[part, :], sh[...],
             (((1,), (1,)), ((), ())), preferred_element_type=jnp.float32,
         ).astype(jnp.bfloat16)
-        send(out.at[part], predicted.at[part])
-        if i == 0:
-            sm_load.wait()
-        turned[lanes, :] = sm[i // per, :, here].T
-        send(turned.at[pl.ds(i * LANES, LANES)], smoothed.at[pl.ds(i * LANES, LANES)])
+        begin(copies, out.at[part], predicted.at[part], sems.at[i])
     for copy in copies:
         copy.wait()
 
@@ -434,7 +463,7 @@
     sm, sh = pl.pallas_call(
         functools.partial(smooth_kernel, n, pn, groups, gw, regimes),
         out_shape=(
-            jax.ShapeDtypeStruct((groups, bins, gw), f32),
+            jax.ShapeDtypeStruct((lat, bins), f32),
             jax.ShapeDtypeStruct((bins, pn * lat), bf16),
         ),
         in_specs=[pl.BlockSpec(memory_space=pl.ANY)] * 6,
@@ -442,7 +471,7 @@
         scratch_shapes=[
             vm((units, bins), bf16),
             vm((bins, units), bf16),
-            vm((pn, units, lat), bf16),
+            vm((pn, groups, units, gw), bf16),
             vm((bins, lat), f32),
             vm((groups, peers, bins, gw), bf16),
             vm((groups, peers, bins, gw), bf16),
@@ -452,15 +481,21 @@
             vm((bins, LANES), jnp.int32),
             vm((CHUNKS, LANES), jnp.int32),
             vm((groups, 13, CHUNKS, LANES), f32),
-            vm((groups, n, ROWS, LANES), f32),
+            vm((groups, 4, CHUNKS, LANES), f32),
+            vm((n, -(-groups * FIXED // 8) * 8, LANES), f32),
+            vm((groups, n, 4, LANES), f32),
             vm((groups, n, 8, LANES), f32),
             vm((groups, 4, CHUNKS, LANES), f32),
             vm((groups, bins, gw), f32),
+            vm((groups, gw, bins), f32),
             vm((groups, bins, gw), bf16),
-            dma((pn + 1,)),
+            dma((units // TURN,)),
+            dma((pn, groups)),
             dma((4,)),
             dma((groups, peers)),
             dma((groups, peers)),
+            dma((n,)),
+            dma((n,)),
             dma((groups, n)),
             dma((groups, n)),
             dma((groups, peers)),
@@ -489,11 +524,9 @@
         scratch_shapes=[
             vm(readout.shape, bf16),
             vm(sh.shape, bf16),
-            vm(sm.shape, f32),
             vm((readout.shape[0], bins), bf16),
-            vm((lat, bins), f32),
-            dma((tiles + 2,)),
-            dma((2 * tiles,)),
+            dma((tiles + 1,)),
+            dma((tiles + 1,)),
         ],
         compiler_params=pltpu.CompilerParams(vmem_limit_bytes=61 * 2**20),
         cost_estimate=pl.CostEstimate(

time: 42.6 us -> 69 us (1.62)
  Pallas kernels: 41.8 us -> 68.2 us
    pallas_call x1, Pallas kernels: 5.66 us -> 33 us  [body(): pl.pallas_call(functools.partial(predict_kernel, tiles), out_shape=(jax.S...]
    pallas_call x1, Pallas kernels: 36.2 us -> 35.2 us  [body(): pl.pallas_call(functools.partial(smooth_kernel, n, pn, groups, gw, regime...]
where the time goes in v3:
time: 69 us; the launch traced here: 68.8 us
  Pallas kernels  68.2 us (99%)
    pallas_call x1, Pallas kernels, body(): pl.pallas_call(functools.partial(smooth_kernel, n, pn, groups, gw, regime...  35.2 us
    pallas_call x1, Pallas kernels, body(): pl.pallas_call(functools.partial(predict_kernel, tiles), out_shape=(jax.S...  33 us

profile of v3, /device:TPU:0, one launch (start us, length us, event | category | flops | bytes accessed | tf_op | source)
XLA Modules:
  0.0 68.8 jit_solution(2063947796859744805)
XLA Ops:
  0.6 35.2 %smooth.1 = (f32[512,512]{1,0:T(8,128)}, bf16[512,1024]{1,0:T(8,128)(2,1)}) custom-call(bf16[2048,512]{1,0:T(8,128)(2,1)} %obs_hbm.1, bf16[2048,1024]{1,0:T(8,128)(2,1)} %w_hbm.1, s32[4,128]{1,0:T(4,128)} %bitcast.1, f32[4,256]{1,0:T(4,128)} %rate_hbm.1, f32[4,256]{1,0:T(4,128)} %angle_hbm.1, f32[4,256]{1,0:T(4,128)} %gain_hbm.1), custom_call_target="tpu_custom_call" | custom-call | flops 2147483648 | bytes 6291456 | tf_op jit(solution)/shard_map/smooth/pallas_call | solution.py:463
  35.9 33.0 %predict.1 = (bf16[2048,512]{1,0:T(8,128)(2,1)}, f32[512,512]{1,0:T(8,128)}) custom-call(bf16[2048,1024]{1,0:T(8,128)(2,1)} %readout_hbm.1, bf16[512,1024]{1,0:T(8,128)(2,1)} %get-tuple-element.6.sh_hbm, f32[512,512]{1,0:T(8,128)} %get-tuple-element.7.sm_hbm), custom_call_target="tpu_custom_call" | custom-call | flops 2147483648 | bytes 8388608 | tf_op jit(solution)/shard_map/predict/pallas_call | solution.py:516

commit v4 on v3

--- a/solution.py
+++ b/solution.py
@@ -206,9 +206,10 @@
     for g in range(groups):
         for s in range(1, pn):
             rs_out[g, s - 1] = project(g, s).astype(jnp.bfloat16)
-            if g == 0 and s == 1:
-                pl.semaphore_wait(barrier, n - 1 + pn - 1)
-            rs_copy(g, s).start()
+            if g == 0:
+                if s == 1:
+                    pl.semaphore_wait(barrier, n - 1 + pn - 1)
+                rs_copy(g, s).start()
 
     def each_peer(act):
         def go(s, _):
@@ -375,19 +376,24 @@
             device_id=(me, panel(s)), device_id_type=MESH,
         )
 
-    def out_copies(g):
-        return (
-            pltpu.make_async_copy(shv.at[g], sh_hbm.at[:, sh_columns(g)], out_sem.at[g, 0]),
-            pltpu.make_async_copy(smt.at[g], sm_hbm.at[pl.ds(g * gw, gw)], out_sem.at[g, 1]),
-        )
+    def sh_copy(g):
+        return pltpu.make_async_copy(shv.at[g], sh_hbm.at[:, sh_columns(g)], out_sem.at[g, 0])
+
+    def sm_copy(g):
+        return pltpu.make_async_copy(smt.at[g], sm_hbm.at[pl.ds(g * gw, gw)], out_sem.at[g, 1])
 
     def turn_out(g):
         for h in range(gw // LANES):
             lanes = slice(h * LANES, (h + 1) * LANES)
             smt[g, lanes, :] = smv[g, :, lanes].T
-        out_copies(g)[1].start()
-
-    for g in range(groups):
+        sm_copy(g).start()
+
+    for g in range(groups):
+        for s in range(1, pn):
+            rs_copy(g, s).wait_send()
+        if g < groups - 1:
+            for s in range(1, pn):
+                rs_copy(g + 1, s).start()
         gather_info(g)
         local_map(g)
         each_peer(lambda s: cm_copy(g, s).start())
@@ -399,21 +405,19 @@
         finish(g)
         for s in range(1, pn):
             ag_copy(g, s).start()
-        out_copies(g)[0].start()
+        sh_copy(g).start()
     turn_out(groups - 1)
     each_peer(lambda s: fx_copy(s).wait_send())
     for g in range(groups):
-        for s in range(1, pn):
-            rs_copy(g, s).wait_send()
         each_peer(lambda s: cm_copy(g, s).wait_send())
-        for copy in out_copies(g):
-            copy.wait()
+        sh_copy(g).wait()
+        sm_copy(g).wait()
         for s in range(1, pn):
             ag_copy(g, s).wait()
 
 
 def predict_kernel(
-    tiles, readout_hbm, sh_hbm, sm_hbm, predicted, smoothed, readout, sh, out, in_sems, sems
+    tiles, readout_hbm, sh_hbm, sm_hbm, predicted, smoothed, readout, sh, sm, out, in_sems, sems
 ):
     rows = readout.shape[0] // tiles
     loads, copies = [], []
@@ -426,7 +430,7 @@
     for i in range(tiles):
         part = pl.ds(i * rows, rows)
         begin(loads, readout_hbm.at[part], readout.at[part], in_sems.at[i])
-    begin(copies, sm_hbm, smoothed, sems.at[tiles])
+    begin(loads, sm_hbm, sm, in_sems.at[tiles + 1])
     loads[0].wait()
     for i in range(tiles):
         part = pl.ds(i * rows, rows)
@@ -436,6 +440,9 @@
             (((1,), (1,)), ((), ())), preferred_element_type=jnp.float32,
         ).astype(jnp.bfloat16)
         begin(copies, out.at[part], predicted.at[part], sems.at[i])
+        if i == 0:
+            loads[-1].wait()
+            begin(copies, sm, smoothed, sems.at[tiles])
     for copy in copies:
         copy.wait()
 
@@ -524,8 +531,9 @@
         scratch_shapes=[
             vm(readout.shape, bf16),
             vm(sh.shape, bf16),
+            vm(sm.shape, f32),
             vm((readout.shape[0], bins), bf16),
-            dma((tiles + 1,)),
+            dma((tiles + 2,)),
             dma((tiles + 1,)),
         ],
         compiler_params=pltpu.CompilerParams(vmem_limit_bytes=61 * 2**20),

time: 69 us -> 41.4 us (0.60)
  Pallas kernels: 68.2 us -> 40.6 us
    pallas_call x1, Pallas kernels: 33 us -> 5.93 us  [body(): pl.pallas_call(functools.partial(predict_kernel, tiles), out_shape=(jax.S...]
where the time goes in v4:
time: 41.4 us; the launch traced here: 41.2 us
  Pallas kernels  40.6 us (98%)
  between operations  0.64 us (2%)
    pallas_call x1, Pallas kernels, body(): pl.pallas_call(functools.partial(smooth_kernel, n, pn, groups, gw, regime...  34.7 us
    pallas_call x1, Pallas kernels, body(): pl.pallas_call(functools.partial(predict_kernel, tiles), out_shape=(jax.S...  5.93 us

profile of v4, /device:TPU:0, one launch (start us, length us, event | category | flops | bytes accessed | tf_op | source)
XLA Modules:
  0.0 41.2 jit_solution(4076969848326015109)
XLA Ops:
  0.6 34.7 %smooth.1 = (f32[512,512]{1,0:T(8,128)}, bf16[512,1024]{1,0:T(8,128)(2,1)}) custom-call(bf16[2048,512]{1,0:T(8,128)(2,1)} %obs_hbm.1, bf16[2048,1024]{1,0:T(8,128)(2,1)} %w_hbm.1, s32[4,128]{1,0:T(4,128)} %bitcast.1, f32[4,256]{1,0:T(4,128)} %rate_hbm.1, f32[4,256]{1,0:T(4,128)} %angle_hbm.1, f32[4,256]{1,0:T(4,128)} %gain_hbm.1), custom_call_target="tpu_custom_call" | custom-call | flops 2147483648 | bytes 6291456 | tf_op jit(solution)/shard_map/smooth/pallas_call | solution.py:470
  35.3 5.9 %predict.1 = (bf16[2048,512]{1,0:T(8,128)(2,1)}, f32[512,512]{1,0:T(8,128)}) custom-call(bf16[2048,1024]{1,0:T(8,128)(2,1)} %readout_hbm.1, bf16[512,1024]{1,0:T(8,128)(2,1)} %get-tuple-element.6.sh_hbm, f32[512,512]{1,0:T(8,128)} %get-tuple-element.7.sm_hbm), custom_call_target="tpu_custom_call" | custom-call | flops 2147483648 | bytes 8388608 | tf_op jit(solution)/shard_map/predict/pallas_call | solution.py:523

commit v5 on v4

--- a/solution.py
+++ b/solution.py
@@ -426,21 +426,27 @@
         into.append(pltpu.make_async_copy(src, dst, sem))
         into[-1].start()
 
+    def fetch(i):
+        part = pl.ds(i * rows, rows)
+        begin(loads, readout_hbm.at[part], readout.at[part], in_sems.at[i])
+
     begin(loads, sh_hbm, sh, in_sems.at[tiles])
+    fetch(0)
+    loads[0].wait()
+    loads[1].wait()
+    for i in range(1, tiles):
+        fetch(i)
+    begin(loads, sm_hbm, sm, in_sems.at[tiles + 1])
     for i in range(tiles):
         part = pl.ds(i * rows, rows)
-        begin(loads, readout_hbm.at[part], readout.at[part], in_sems.at[i])
-    begin(loads, sm_hbm, sm, in_sems.at[tiles + 1])
-    loads[0].wait()
-    for i in range(tiles):
-        part = pl.ds(i * rows, rows)
-        loads[i + 1].wait()
+        if i:
+            loads[i + 1].wait()
         out[part, :] = lax.dot_general(
             readout[part, :], sh[...],
             (((1,), (1,)), ((), ())), preferred_element_type=jnp.float32,
         ).astype(jnp.bfloat16)
         begin(copies, out.at[part], predicted.at[part], sems.at[i])
-        if i == 0:
+        if i == tiles // 2:
             loads[-1].wait()
             begin(copies, sm, smoothed, sems.at[tiles])
     for copy in copies:

time: 41.4 us -> 41.3 us (level)
  no operation moved by 1% of the time
where the time goes in v5:
time: 41.3 us; the launch traced here: 41.2 us
  Pallas kernels  40.6 us (98%)
  between operations  0.64 us (2%)
    pallas_call x1, Pallas kernels, body(): pl.pallas_call(functools.partial(smooth_kernel, n, pn, groups, gw, regime...  34.7 us
    pallas_call x1, Pallas kernels, body(): pl.pallas_call(functools.partial(predict_kernel, tiles), out_shape=(jax.S...  5.89 us

profile of v5, /device:TPU:0, one launch (start us, length us, event | category | flops | bytes accessed | tf_op | source)
XLA Modules:
  0.0 41.2 jit_solution(10053910994776706541)
XLA Ops:
  0.6 34.7 %smooth.1 = (f32[512,512]{1,0:T(8,128)}, bf16[512,1024]{1,0:T(8,128)(2,1)}) custom-call(bf16[2048,512]{1,0:T(8,128)(2,1)} %obs_hbm.1, bf16[2048,1024]{1,0:T(8,128)(2,1)} %w_hbm.1, s32[4,128]{1,0:T(4,128)} %bitcast.1, f32[4,256]{1,0:T(4,128)} %rate_hbm.1, f32[4,256]{1,0:T(4,128)} %angle_hbm.1, f32[4,256]{1,0:T(4,128)} %gain_hbm.1), custom_call_target="tpu_custom_call" | custom-call | flops 2147483648 | bytes 6291456 | tf_op jit(solution)/shard_map/smooth/pallas_call | solution.py:476
  35.3 5.9 %predict.1 = (bf16[2048,512]{1,0:T(8,128)(2,1)}, f32[512,512]{1,0:T(8,128)}) custom-call(bf16[2048,1024]{1,0:T(8,128)(2,1)} %readout_hbm.1, bf16[512,1024]{1,0:T(8,128)(2,1)} %get-tuple-element.6.sh_hbm, f32[512,512]{1,0:T(8,128)} %get-tuple-element.7.sm_hbm), custom_call_target="tpu_custom_call" | custom-call | flops 2147483648 | bytes 8388608 | tf_op jit(solution)/shard_map/predict/pallas_call | solution.py:529
